TPU v7x, 32 devices: a whole 2x2x4 slice. The times are simulated.
32 devices in a mesh: groups: 2 (over y), row: 4 (over x, core), col: 4 (over z).
Axes of the slice: x: 2, y: 2, z: 4, core: 2. Of those that a mesh axis runs over, the one named last changes fastest.
Arguments:
- basis_values: bfloat16 [4, 4, 2048, 1536], P('row', 'col'), may hold values from -6 to 6
- potential: float32 [4, 4, 2048], P('row', 'col'), may hold values from -0.125 to 0.125
- basis_blocks: int32 [4, 4, 12], P('row', 'col'), may hold values from 0 to 63, as said below
- factor: bfloat16 [16, 4, 128, 1024], P(None, 'row', None, 'col'), may hold values from -0.1875 to 0.1875
Outputs:
- hamiltonian: float32 [32, 4, 16, 4, 128, 128], P('groups', 'row', None, 'col'), parts along dimension 0
- product: float32 [32, 4, 128, 16, 4, 128], P('groups', 'row', None, None, 'col'), parts along dimension 0
There are 2 independent parts, one for each index of `groups`. A program takes and returns all parts, laid end to end along the dimension named above; an argument that names none is the same for every part. Nothing has to cross between parts.
Inputs may be any that keep to these rules, and one draw needn't show every extreme that they name: `basis_blocks`: the 12 blocks of one batch are distinct and lie within 16 consecutive blocks counted cyclically over the 64 blocks of the window; every such range starts at one common offset modulo 16, and every block of the range whose position in it is a multiple of 4 is on the list. Hence at most 16 of a batch's block pairs (I, J) share the same (I mod 4, J mod 4), and some pair of residues has exactly 16.
All inputs are finite; a program needn't handle non-finite values.
Results may differ from a plain program's by a relative error of at most 0.0048.
Values may be sent and summed in bfloat16 or wider, within the bound.
A program may use at most 128 MiB of HBM per device.

v0:
```python
import jax
import jax.numpy as jnp
from jax import lax
from jax.sharding import PartitionSpec as P

NB = 8192
WIN = 16


def from_root(value, axis, source):
    kept = jnp.where(lax.axis_index(axis) == source, value, 0).astype(value.dtype)
    return lax.psum(kept, axis)


def slot_ranks(targets, usable):
    count = targets.shape[0]
    order = jnp.arange(count)
    earlier = order[None, :] < order[:, None]
    same_target = (targets[:, None] == targets[None, :]) & usable[None, :] & earlier
    return jnp.sum(same_target.astype(jnp.int32), axis=1)


def pack_slots(slot_of_item, slot_count, items, labels):
    selector = jnp.arange(slot_count)[:, None] == slot_of_item[None, :]
    packed = jnp.dot(
        selector.astype(jnp.bfloat16), items, preferred_element_type=jnp.float32
    ).astype(jnp.bfloat16)
    slot_labels = jnp.sum(jnp.where(selector, labels[None, :] + 1, 0), axis=1) - 1
    return (packed, slot_labels)


def sum_into_tile(received, received_labels, tile_blocks):
    selector = received_labels[:, None] == jnp.arange(tile_blocks)[None, :]
    return lax.dot_general(
        selector.astype(jnp.bfloat16),
        received,
        (((0,), (0,)), ((), ())),
        preferred_element_type=jnp.float32,
    )


def local(basis_values, potential, basis_blocks, factor):
    row_count = lax.axis_size("row")
    col_count = lax.axis_size("col")
    device_count = row_count * col_count
    phi_batch = basis_values[0, 0]
    weight_batch = potential[0, 0]
    block_list = basis_blocks[0, 0]
    list_length = block_list.shape[0]
    block_size = factor.shape[2]
    block_area = block_size * block_size
    window = WIN
    total_blocks = NB // block_size
    local_rows = total_blocks // row_count
    local_cols = total_blocks // col_count
    tile_blocks = local_rows * local_cols
    weighted = (phi_batch * weight_batch[:, None]).astype(jnp.bfloat16)
    partial_sum = lax.dot_general(
        phi_batch, weighted, (((0,), (0,)), ((), ())), preferred_element_type=jnp.float32
    ).astype(jnp.bfloat16)
    pieces = partial_sum.reshape(list_length, block_size, list_length, block_size).transpose(
        0, 2, 1, 3
    )
    row_share = min(list_length, window // row_count)
    col_share = min(list_length, window // col_count)
    row_label = jnp.broadcast_to(block_list[:, None], (list_length, list_length)).reshape(-1)
    col_label = jnp.broadcast_to(block_list[None, :], (list_length, list_length)).reshape(-1)
    owner = row_label % row_count * col_count + col_label % col_count
    capacity = row_share * col_share
    usable = jnp.ones(owner.shape, bool)
    slot_of_item = owner * capacity + slot_ranks(owner, usable)
    local_label = row_label // row_count * local_cols + col_label // col_count
    packed, slot_labels = pack_slots(
        slot_of_item,
        device_count * capacity,
        pieces.reshape(list_length * list_length, block_area),
        local_label,
    )
    packed = packed.reshape(device_count, capacity, block_area)
    slot_labels = slot_labels.reshape(device_count, capacity)
    received, received_labels = (
        lax.all_to_all(packed, ("row", "col"), split_axis=0, concat_axis=0, tiled=True),
        lax.all_to_all(slot_labels, ("row", "col"), split_axis=0, concat_axis=0, tiled=True),
    )
    tile = sum_into_tile(received.reshape(-1, block_area), received_labels.reshape(-1), tile_blocks)
    tile = tile.reshape(local_rows, local_cols, block_size, block_size)
    hamiltonian = tile.reshape(local_rows, 1, local_cols, 1, block_size, block_size)
    tile_narrow = tile.astype(jnp.bfloat16)
    head_width = factor.shape[3] * col_count
    head_blocks = head_width // block_size
    gathered_rows = []
    for block_row in range(head_blocks):
        gathered_rows.append(
            from_root(tile_narrow[block_row // row_count], "row", block_row % row_count)
        )
    head_stack = jnp.stack(gathered_rows, axis=0)
    head_matrix = head_stack.transpose(0, 2, 1, 3).reshape(head_width, local_cols * block_size)
    piece = lax.all_gather(factor, "col", axis=3, tiled=True)
    width = piece.shape[3]
    product = jnp.dot(
        piece.reshape(local_rows * block_size, width),
        head_matrix,
        preferred_element_type=jnp.float32,
    )
    product = product.reshape(local_rows, 1, block_size, local_cols, 1, block_size)
    return (hamiltonian, product)


def solution(mesh):
    return jax.shard_map(
        local,
        mesh=mesh,
        in_specs=(
            P("row", "col", None, None),
            P("row", "col", None),
            P("row", "col", None),
            P(None, "row", None, "col"),
        ),
        out_specs=(
            P("groups", "row", None, "col", None, None),
            P("groups", "row", None, None, "col", None),
        ),
        check_vma=False,
    )
```

profile of v0, /device:TPU:0, one launch (start us, length us, event | category | flops | bytes accessed | tf_op | source)
XLA Modules:
  0.0 423.9 jit_solution(7756939959881441454)
XLA Ops:
  8.0 0.7 broadcast_in_dim.45
  8.7 0.1 reshape.286
  8.7 0.7 broadcast_in_dim.44
  9.5 0.1 reshape.285
  9.6 0.2 convert_reduce_fusion
  9.8 0.1 select_reduce_fusion
  9.9 0.7 sub.19
  10.6 7.4 %all-to-all-start = ((s32[16,1,16]{2,1,0:T(1,128)}), s32[16,1,16]{2,1,0:T(1,128)S(1)}, u32[]{:S(2)}, u32[]{:S(2)}) async-start(s32[16,1,16]{2,1,0:T(1,128)} %sub.19), calls=%async_computation | async-start | bytes 16384 | tf_op jit(solution)/shard_map/all_to_all | solution.py:83
  18.0 15.6 %fusion = bf16[1536,1536]{0,1:T(8,128)(2,1)} fusion(bf16[1,1,2048,1536]{3,2,1,0:T(8,128)(2,1)} %param.4, f32[2048]{0:T(1024)} %bitcast.89), kind=kOutput, calls=%fused_computation.4 | convolution fusion | flops 9675472896 | bytes 11018240 | tf_op jit(solution)/shard_map/dot_general | solution.py:58
  33.6 6.6 %copy.20 = bf16[1536,1536]{1,0:T(8,128)(2,1)} copy(bf16[1536,1536]{0,1:T(8,128)(2,1)} %fusion) | data formatting | bytes 9437184 | tf_op jit(solution)/shard_map/convert_element_type | solution.py:60
  40.2 9.4 %reshape.287 = bf16[12,128,12,128]{3,2,1,0:T(8,128)(2,1)} reshape(bf16[1536,1536]{1,0:T(8,128)(2,1)} %copy.20) | data formatting | bytes 9437184 | tf_op jit(solution)/shard_map/reshape | solution.py:61
  49.6 4.1 copy.21
  53.8 7.4 %convolution_convert_fusion = bf16[256,16384]{1,0:T(8,128)(2,1)} fusion(bf16[18,8,128,128]{3,2,1,0:T(8,128)(2,1)S(1)} %bitcast.76, s32[144]{0:T(256)S(1)} %multiply_add_fusion), kind=kOutput, calls=%fused_computation | convolution fusion | flops 1212190720 | bytes 13107776 | tf_op jit(solution)/shard_map/dot_general | solution.py:25
  61.2 0.0 all-to-all-done
  61.2 6.1 %all-to-all-start.1 = ((bf16[16,16,16384]{2,1,0:T(8,128)(2,1)}), bf16[16,16,16384]{2,1,0:T(8,128)(2,1)}, u32[]{:S(2)}, u32[]{:S(2)}) async-start(bf16[16,16,16384]{2,1,0:T(8,128)(2,1)} %bitcast.74), calls=%async_computation.1 | async-start | bytes 16777216 | tf_op jit(solution)/shard_map/all_to_all | solution.py:82
  67.3 0.2 all-reduce.3.cloned.1.call-start
  67.5 0.5 broadcast.328
  68.0 0.7 reduce.3
  68.7 0.1 eq.66
  68.8 182.8 %all-to-all-done.1 = bf16[16,16,16384]{2,1,0:T(8,128)(2,1)} async-done(((bf16[16,16,16384]{2,1,0:T(8,128)(2,1)}), bf16[16,16,16384]{2,1,0:T(8,128)(2,1)}, u32[]{:S(2)}, u32[]{:S(2)}) %all-to-all-start.1) | async-done | bytes 8388640 | tf_op jit(solution)/shard_map/all_to_all | solution.py:82
  251.6 12.0 %fusion.17 = (bf16[256,16384]{1,0:T(8,128)(2,1)S(1)}, f32[256,16384]{1,0:T(8,128)}) fusion(bf16[256,16384]{1,0:T(8,128)(2,1)} %bitcast.7, s32[256]{0:T(256)S(1)} %eq.66), kind=kOutput, calls=%fused_computation.57 | convolution fusion | flops 2151743488 | bytes 33555456 | tf_op jit(solution)/shard_map/dot_general | solution.py:34
  263.6 0.3 select_bitcast_fusion
  263.9 0.1 copy.41
  264.0 1.2 copy.29
  265.1 0.1 copy.35
  265.2 1.2 copy.23
  266.4 0.1 copy.36
  266.5 1.1 copy.24
  267.6 0.1 copy.39
  267.7 1.1 copy.27
  268.9 0.1 copy.40
  269.0 1.1 copy.28
  270.1 0.1 copy.38
  270.2 1.2 copy.26
  271.3 0.1 copy.34
  271.4 1.2 copy.22
  272.6 0.1 copy.37
  272.7 1.1 copy.25
  273.8 0.0 all-reduce.3.cloned.1.call-update
  273.9 0.3 all-gather.2.cloned.1.call-start
  274.1 0.3 all-gather.2.cloned.1.call-update
  274.4 14.3 %copy.33 = f32[32,8,128,128]{3,2,1,0:T(8,128)} copy(f32[32,8,128,128]{3,1,2,0:T(8,128)} %bitcast.72) | data formatting | bytes 33554432
  288.8 70.7 %all-reduce.3.cloned.1.call-done = (bf16[1,16,128,128]{3,1,2,0:T(8,128)(2,1)}, bf16[1,16,128,128]{3,1,2,0:T(8,128)(2,1)}, bf16[1,16,128,128]{3,1,2,0:T(8,128)(2,...) async-done(((bf16[1,16,128,128]{3,1,2,0:T(8,128)(2,1)}, ...) | async-done | bytes 4194320 | tf_op jit(solution)/shard_map/psum | solution.py:12
  359.5 0.0 copy-start.2
  359.5 0.0 copy-start.1
  359.5 0.0 copy-start
  359.5 2.0 constant_dynamic-update-slice_fusion.7
  361.5 1.9 constant_dynamic-update-slice_fusion.6
  363.3 1.9 constant_dynamic-update-slice_fusion.5
  365.2 1.9 constant_dynamic-update-slice_fusion.4
  367.1 1.9 constant_dynamic-update-slice_fusion.3
  368.9 0.0 copy-done.2
  368.9 0.8 constant_dynamic-update-slice_fusion.2
  369.8 0.0 copy-done.1
  369.8 0.8 constant_dynamic-update-slice_fusion.1
  370.6 0.0 copy-done
  370.6 0.8 constant_dynamic-update-slice_fusion
  371.4 0.0 all-gather.2.cloned.1.call-done
  371.4 12.6 %convolution_bitcast_fusion = f32[256,8,16,128]{3,1,2,0:T(8,128)S(1)} fusion(bf16[2048,1024]{1,0:T(8,128)(2,1)} %bitcast.88, bf16[128,8,16,128]{3,2,1,0:T(8,128)(2,1)} %bitcast.44), kind=kOutput, calls=%fused_computation.2 | convolution fusion | flops 8589934592 | bytes 25165824 | tf_op jit(solution)/shard_map/dot_general | solution.py:100
  384.0 7.5 %copy.43 = f32[256,8,16,128]{3,2,1,0:T(8,128)} copy(f32[256,8,16,128]{3,1,2,0:T(8,128)S(1)} %convolution_bitcast_fusion) | data formatting | bytes 33554432
  391.5 24.9 %copy.31 = f32[16,1,128,16,1,128]{5,4,3,2,1,0:T(1,128)} copy(f32[16,1,128,16,1,128]{2,0,5,3,4,1:T(8,128)} %bitcast.73) | data formatting | bytes 33554432
  (3 shorter events, 0.0 us)
Async XLA Ops:
  10.6 50.6 %all-to-all-start = ((s32[16,1,16]{2,1,0:T(1,128)}), s32[16,1,16]{2,1,0:T(1,128)S(1)}, u32[]{:S(2)}, u32[]{:S(2)}) async-start(s32[16,1,16]{2,1,0:T(1,128)} %sub.19), calls=%async_computation | async-start | bytes 16384 | tf_op jit(solution)/shard_map/all_to_all | solution.py:83
  61.2 190.4 %all-to-all-start.1 = ((bf16[16,16,16384]{2,1,0:T(8,128)(2,1)}), bf16[16,16,16384]{2,1,0:T(8,128)(2,1)}, u32[]{:S(2)}, u32[]{:S(2)}) async-start(bf16[16,16,16384]{2,1,0:T(8,128)(2,1)} %bitcast.74), calls=%async_computation.1 | async-start | bytes 16777216 | tf_op jit(solution)/shard_map/all_to_all | solution.py:82
  67.3 292.2 %all-reduce.3.cloned.1.call-start = ((), (), s32[]{:S(2)}) async-start(), calls=%async_computation.3 | async-start | bytes 8388608 | tf_op jit(solution)/shard_map/psum | solution.py:12
  273.9 97.6 %all-gather.2.cloned.1.call-start = ((), (), s32[]{:S(2)}) async-start(), calls=%async_computation.2 | async-start | bytes 5242880 | tf_op jit(solution)/shard_map/all_gather | solution.py:98
  359.5 9.5 %copy-start.2 = (bf16[1,16,128,128]{3,1,2,0:T(8,128)(2,1)S(1)}, bf16[1,16,128,128]{3,1,2,0:T(8,128)(2,1)}, u32[]{:S(2)}) copy-start(bf16[1,16,128,128]{3,1,2,0:T(8,128)(2,1)} %get-tuple-element.13) | copy-start | bytes 1572868
  359.5 10.3 %copy-start.1 = (bf16[1,16,128,128]{3,1,2,0:T(8,128)(2,1)S(1)}, bf16[1,16,128,128]{3,1,2,0:T(8,128)(2,1)}, u32[]{:S(2)}) copy-start(bf16[1,16,128,128]{3,1,2,0:T(8,128)(2,1)} %get-tuple-element.14) | copy-start | bytes 1572868
  359.5 11.1 %copy-start = (bf16[1,16,128,128]{3,1,2,0:T(8,128)(2,1)S(1)}, bf16[1,16,128,128]{3,1,2,0:T(8,128)(2,1)}, u32[]{:S(2)}) copy-start(bf16[1,16,128,128]{3,1,2,0:T(8,128)(2,1)} %get-tuple-element.15) | copy-start | bytes 1572868
Sparse Core Ops, SparseCore 0:
  274.0 85.4 all-reduce.2
Sparse Core Ops, SparseCore 1:
  275.9 79.1 all-gather.1
where the time goes:
time: 425 us; the launch traced here: 424 us
  waiting for transfers between devices  254 us (60%)
  local copies, waits for them, and re-layouts  91.6 us (22%)
  matrix products  47.6 us (11%)
  between operations  15.6 us (4%)
  starting transfers between devices  13.9 us (3%)
    all_to_all x1, waiting for transfers between devices, local(): lax.all_to_all(packed, ('row', 'col'), split_axis=0, concat_axis=0, tiled...  183 us
    psum x1, waiting for transfers between devices, from_root(): return lax.psum(kept, axis)  70.7 us
    unnamed x24, local copies, waits for them, and re-layouts  58.6 us
    dot_general x1, matrix products, local(): lax.dot_general(phi_batch, weighted, (((0,), (0,)), ((), ())), preferred_...  15.6 us
    dot_general x1, matrix products, local(): jnp.dot(piece.reshape(local_rows * block_size, width), head_matrix, prefe...  12.6 us
    dot_general x1, matrix products, sum_into_tile(): lax.dot_general(selector.astype(jnp.bfloat16), received, (((0,), (0,)), (...  12 us
    another operation x9, local copies, waits for them, and re-layouts, local(): head_stack = jnp.stack(gathered_rows, axis=0)  10 us
    reshape x1, local copies, waits for them, and re-layouts, local(): partial_sum.reshape(list_length, block_size, list_length, block_size)  9.42 us
  transfers between devices with their start and end apart: 4, of which 2 were waited for; matrix products, arithmetic and copies ran while one was open for 17% of the time, Pallas kernels for 0%

commit v1 on v0

--- a/solution.py
+++ b/solution.py
@@ -9,7 +9,7 @@
 
 def from_root(value, axis, source):
     kept = jnp.where(lax.axis_index(axis) == source, value, 0).astype(value.dtype)
-    return lax.psum(kept, axis)
+    return jnp.sum(lax.all_gather(kept, axis), axis=0)
 
 
 def slot_ranks(targets, usable):

time: 425 us -> 590 us (1.39)
  waiting for transfers between devices: 254 us -> 408 us
  other arithmetic: 1.28 us -> 20.1 us
  local copies, waits for them, and re-layouts: 91.6 us -> 85.3 us
    all_gather x0 -> x8, waiting for transfers between devices: none -> 152 us  [from_root(): return jnp.sum(lax.all_gather(kept, axis), axis=0)]
    all_gather x1, waiting for transfers between devices: 0.01 us -> 71.7 us  [local(): piece = lax.all_gather(factor, 'col', axis=3, tiled=True)]
    psum x1 -> x0, waiting for transfers between devices: 70.7 us -> none  [from_root(): return lax.psum(kept, axis)]
    reduce_sum x0 -> x8, other arithmetic: none -> 18 us  [from_root(): return jnp.sum(lax.all_gather(kept, axis), axis=0)]
    another operation x9 -> x1, local copies, waits for them, and re-layouts: 10 us -> 0.07 us  [local(): head_stack = jnp.stack(gathered_rows, axis=0)]
    unnamed x24 -> x18, local copies, waits for them, and re-layouts: 58.6 us -> 57.4 us
  transfers between devices with their start and end apart: 4 -> 11, of which waited for: 2 -> 9; matrix products, arithmetic and copies ran while one was open for 17% -> 16% of each run, Pallas kernels for 0% -> 0%
where the time goes in v1:
time: 590 us; the launch traced here: 589 us
  waiting for transfers between devices  408 us (69%)
  local copies, waits for them, and re-layouts  85.3 us (14%)
  matrix products  47.6 us (8%)
  other arithmetic  20.1 us (3%)
  starting transfers between devices  14 us (2%)
  between operations  14 us (2%)
    all_to_all x1, waiting for transfers between devices, local(): lax.all_to_all(packed, ('row', 'col'), split_axis=0, concat_axis=0, tiled...  183 us
    all_gather x8, waiting for transfers between devices, from_root(): return jnp.sum(lax.all_gather(kept, axis), axis=0)  152 us
    all_gather x1, waiting for transfers between devices, local(): piece = lax.all_gather(factor, 'col', axis=3, tiled=True)  71.7 us
    unnamed x18, local copies, waits for them, and re-layouts  57.4 us
    reduce_sum x8, other arithmetic, from_root(): return jnp.sum(lax.all_gather(kept, axis), axis=0)  18 us
    dot_general x1, matrix products, local(): lax.dot_general(phi_batch, weighted, (((0,), (0,)), ((), ())), preferred_...  15.6 us
    dot_general x1, matrix products, local(): jnp.dot(piece.reshape(local_rows * block_size, width), head_matrix, prefe...  12.6 us
    dot_general x1, matrix products, sum_into_tile(): lax.dot_general(selector.astype(jnp.bfloat16), received, (((0,), (0,)), (...  12 us
  transfers between devices with their start and end apart: 11, of which 9 were waited for; matrix products, arithmetic and copies ran while one was open for 16% of the time, Pallas kernels for 0%

profile of v1, /device:TPU:0, one launch (start us, length us, event | category | flops | bytes accessed | tf_op | source)
XLA Modules:
  0.0 588.7 jit_solution(6911053354208654765)
XLA Ops:
  7.2 0.7 broadcast_in_dim.45
  7.8 0.1 reshape.254
  7.9 0.7 broadcast_in_dim.44
  8.6 0.1 reshape.253
  8.7 0.2 convert_reduce_fusion
  8.9 0.1 select_reduce_fusion
  9.1 0.7 sub.19
  9.8 7.4 %all-to-all-start = ((s32[16,1,16]{2,1,0:T(1,128)}), s32[16,1,16]{2,1,0:T(1,128)S(1)}, u32[]{:S(2)}, u32[]{:S(2)}) async-start(s32[16,1,16]{2,1,0:T(1,128)} %sub.19), calls=%async_computation | async-start | bytes 16384 | tf_op jit(solution)/shard_map/all_to_all | solution.py:83
  17.1 15.6 %fusion = bf16[1536,1536]{0,1:T(8,128)(2,1)} fusion(bf16[1,1,2048,1536]{3,2,1,0:T(8,128)(2,1)} %param.4, f32[2048]{0:T(1024)} %bitcast.107), kind=kOutput, calls=%fused_computation.4 | convolution fusion | flops 9675472896 | bytes 11018240 | tf_op jit(solution)/shard_map/dot_general | solution.py:58
  32.8 6.6 %copy.17 = bf16[1536,1536]{1,0:T(8,128)(2,1)} copy(bf16[1536,1536]{0,1:T(8,128)(2,1)} %fusion) | data formatting | bytes 9437184 | tf_op jit(solution)/shard_map/convert_element_type | solution.py:60
  39.4 9.4 %reshape.255 = bf16[12,128,12,128]{3,2,1,0:T(8,128)(2,1)} reshape(bf16[1536,1536]{1,0:T(8,128)(2,1)} %copy.17) | data formatting | bytes 9437184 | tf_op jit(solution)/shard_map/reshape | solution.py:61
  48.8 4.1 copy.18
  52.9 7.4 %convolution_convert_fusion = bf16[256,16384]{1,0:T(8,128)(2,1)} fusion(bf16[18,8,128,128]{3,2,1,0:T(8,128)(2,1)S(1)} %bitcast.92, s32[144]{0:T(256)S(1)} %multiply_add_fusion), kind=kOutput, calls=%fused_computation | convolution fusion | flops 1212190720 | bytes 13107776 | tf_op jit(solution)/shard_map/dot_general | solution.py:25
  60.4 6.1 %all-to-all-start.1 = ((bf16[16,16,16384]{2,1,0:T(8,128)(2,1)}), bf16[16,16,16384]{2,1,0:T(8,128)(2,1)}, u32[]{:S(2)}, u32[]{:S(2)}) async-start(bf16[16,16,16384]{2,1,0:T(8,128)(2,1)} %bitcast.90), calls=%async_computation.1 | async-start | bytes 16777216 | tf_op jit(solution)/shard_map/all_to_all | solution.py:82
  66.4 0.2 all-gather.24.cloned.1.call-start
  66.7 0.5 broadcast.312
  67.2 0.7 reduce.11
  67.8 0.1 eq.66
  67.9 182.8 %all-to-all-done.1 = bf16[16,16,16384]{2,1,0:T(8,128)(2,1)} async-done(((bf16[16,16,16384]{2,1,0:T(8,128)(2,1)}), bf16[16,16,16384]{2,1,0:T(8,128)(2,1)}, u32[]{:S(2)}, u32[]{:S(2)}) %all-to-all-start.1) | async-done | bytes 8388640 | tf_op jit(solution)/shard_map/all_to_all | solution.py:82
  250.7 12.0 %fusion.17 = (bf16[256,16384]{1,0:T(8,128)(2,1)S(1)}, f32[256,16384]{1,0:T(8,128)}) fusion(bf16[256,16384]{1,0:T(8,128)(2,1)} %bitcast.7, s32[256]{0:T(256)S(1)} %eq.66), kind=kOutput, calls=%fused_computation.57 | convolution fusion | flops 2151743488 | bytes 33555456 | tf_op jit(solution)/shard_map/dot_general | solution.py:34
  262.7 1.1 select_bitcast_fusion
  263.8 0.9 copy.31
  264.7 0.0 all-gather.12.cloned.1.call-start
  264.8 1.9 copy.25
  266.8 0.0 all-gather.14.cloned.1.call-start
  266.8 0.9 copy.26
  267.8 0.0 all-gather.20.cloned.1.call-start
  267.8 0.9 copy.29
  268.7 0.0 all-gather.22.cloned.1.call-start
  268.8 0.9 copy.30
  269.7 0.9 copy.28
  270.7 0.9 copy.24
  271.6 0.0 all-gather.16.cloned.1.call-start
  271.7 0.9 copy.27
  272.7 0.7 all-gather.26.cloned.1.call-update
  273.4 14.2 %copy.23 = f32[32,8,128,128]{3,2,1,0:T(8,128)} copy(f32[32,8,128,128]{3,1,2,0:T(8,128)} %bitcast.88) | data formatting | bytes 33554432
  287.5 2.0 reduce_sum.123
  289.6 20.8 %all-gather.12.cloned.1.call-done = bf16[4,16,128,128]{3,2,1,0:T(8,128)(2,1)} async-done(((bf16[1,16,128,128]{3,2,1,0:T(8,128)(2,1)}), bf16[4,16,128,128]{3,2,1,0:T(8,128)(2,1)}) %all-gather.12.cloned.1.call-update) | async-done | bytes 2097168 | tf_op jit(solution)/shard_map/all_gather | solution.py:12
  310.3 2.0 reduce_sum.117
  312.4 22.2 %all-gather.14.cloned.1.call-done = bf16[4,16,128,128]{3,2,1,0:T(8,128)(2,1)} async-done(((bf16[1,16,128,128]{3,2,1,0:T(8,128)(2,1)}), bf16[4,16,128,128]{3,2,1,0:T(8,128)(2,1)}) %all-gather.14.cloned.1.call-update) | async-done | bytes 2097168 | tf_op jit(solution)/shard_map/all_gather | solution.py:12
  334.5 2.0 reduce_sum.118
  336.5 22.0 %all-gather.20.cloned.1.call-done = bf16[4,16,128,128]{3,2,1,0:T(8,128)(2,1)} async-done(((bf16[1,16,128,128]{3,2,1,0:T(8,128)(2,1)}), bf16[4,16,128,128]{3,2,1,0:T(8,128)(2,1)}) %all-gather.20.cloned.1.call-update) | async-done | bytes 2097168 | tf_op jit(solution)/shard_map/all_gather | solution.py:12
  358.6 2.0 reduce_sum.121
  360.6 22.0 %all-gather.22.cloned.1.call-done = bf16[4,16,128,128]{3,2,1,0:T(8,128)(2,1)} async-done(((bf16[1,16,128,128]{3,2,1,0:T(8,128)(2,1)}), bf16[4,16,128,128]{3,2,1,0:T(8,128)(2,1)}) %all-gather.22.cloned.1.call-update) | async-done | bytes 2097168 | tf_op jit(solution)/shard_map/all_gather | solution.py:12
  382.6 2.0 reduce_sum.122
  384.6 22.0 %all-gather.18.cloned.1.call-done = bf16[4,16,128,128]{3,2,1,0:T(8,128)(2,1)} async-done(((bf16[1,16,128,128]{3,2,1,0:T(8,128)(2,1)}), bf16[4,16,128,128]{3,2,1,0:T(8,128)(2,1)}) %all-gather.18.cloned.1.call-update) | async-done | bytes 2097168 | tf_op jit(solution)/shard_map/all_gather | solution.py:12
  406.6 2.0 reduce_sum.120
  408.6 22.2 %all-gather.10.cloned.1.call-done = bf16[4,16,128,128]{3,2,1,0:T(8,128)(2,1)} async-done(((bf16[1,16,128,128]{3,2,1,0:T(8,128)(2,1)}), bf16[4,16,128,128]{3,2,1,0:T(8,128)(2,1)}) %all-gather.10.cloned.1.call-update) | async-done | bytes 2097168 | tf_op jit(solution)/shard_map/all_gather | solution.py:12
  430.8 2.9 reduce_sum.116
  433.7 21.3 %all-gather.16.cloned.1.call-done = bf16[4,16,128,128]{3,2,1,0:T(8,128)(2,1)} async-done(((bf16[1,16,128,128]{3,2,1,0:T(8,128)(2,1)}), bf16[4,16,128,128]{3,2,1,0:T(8,128)(2,1)}) %all-gather.16.cloned.1.call-update) | async-done | bytes 2097168 | tf_op jit(solution)/shard_map/all_gather | solution.py:12
  455.0 2.9 reduce_sum.119
  457.9 1.1 bitcast_dynamic-update-slice_fusion.7
  459.0 0.1 bitcast_dynamic-update-slice_fusion.6
  459.1 0.1 bitcast_dynamic-update-slice_fusion.5
  459.1 1.1 bitcast_dynamic-update-slice_fusion.4
  460.3 0.1 bitcast_dynamic-update-slice_fusion.3
  460.4 0.1 bitcast_dynamic-update-slice_fusion.2
  460.4 0.1 bitcast_dynamic-update-slice_fusion.1
  460.5 0.1 bitcast_dynamic-update-slice_fusion
  460.6 4.9 copy.19
  465.4 71.7 %all-gather.26.cloned.1.call-done = bf16[16,1,128,1024]{3,2,1,0:T(8,128)(2,1)} async-done(((bf16[16,1,128,256]{3,2,1,0:T(8,128)(2,1)}), bf16[16,1,128,1024]{3,2,1,0:T(8,128)(2,1)}) %all-gather.26.cloned.1.call-update) | async-done | bytes 4194320 | tf_op jit(solution)/shard_map/all_gather | solution.py:98
  537.2 12.6 %convolution_bitcast_fusion = f32[256,8,16,128]{3,1,2,0:T(8,128)S(1)} fusion(bf16[2048,1024]{1,0:T(8,128)(2,1)} %bitcast.106, bf16[128,8,16,128]{3,2,1,0:T(8,128)(2,1)} %bitcast.95), kind=kOutput, calls=%fused_computation.2 | convolution fusion | flops 8589934592 | bytes 25165824 | tf_op jit(solution)/shard_map/dot_general | solution.py:100
  549.8 7.5 %copy.33 = f32[256,8,16,128]{3,2,1,0:T(8,128)} copy(f32[256,8,16,128]{3,1,2,0:T(8,128)S(1)} %convolution_bitcast_fusion) | data formatting | bytes 33554432
  557.3 24.9 %copy.21 = f32[16,1,128,16,1,128]{5,4,3,2,1,0:T(1,128)} copy(f32[16,1,128,16,1,128]{2,0,5,3,4,1:T(8,128)} %bitcast.89) | data formatting | bytes 33554432
  (16 shorter events, 0.3 us)
Async XLA Ops:
  9.8 50.6 %all-to-all-start = ((s32[16,1,16]{2,1,0:T(1,128)}), s32[16,1,16]{2,1,0:T(1,128)S(1)}, u32[]{:S(2)}, u32[]{:S(2)}) async-start(s32[16,1,16]{2,1,0:T(1,128)} %sub.19), calls=%async_computation | async-start | bytes 16384 | tf_op jit(solution)/shard_map/all_to_all | solution.py:83
  60.4 190.4 %all-to-all-start.1 = ((bf16[16,16,16384]{2,1,0:T(8,128)(2,1)}), bf16[16,16,16384]{2,1,0:T(8,128)(2,1)}, u32[]{:S(2)}, u32[]{:S(2)}) async-start(bf16[16,16,16384]{2,1,0:T(8,128)(2,1)} %bitcast.90), calls=%async_computation.1 | async-start | bytes 16777216 | tf_op jit(solution)/shard_map/all_to_all | solution.py:82
  66.4 221.1 %all-gather.24.cloned.1.call-start = ((), (), s32[]{:S(2)}) async-start(), calls=%async_computation.9 | async-start | bytes 2621440 | tf_op jit(solution)/shard_map/all_gather | solution.py:12
  264.7 45.6 %all-gather.12.cloned.1.call-start = ((), (), s32[]{:S(2)}) async-start(), calls=%async_computation.3 | async-start | bytes 2621440 | tf_op jit(solution)/shard_map/all_gather | solution.py:12
  266.8 67.7 %all-gather.14.cloned.1.call-start = ((), (), s32[]{:S(2)}) async-start(), calls=%async_computation.4 | async-start | bytes 2621440 | tf_op jit(solution)/shard_map/all_gather | solution.py:12
  267.8 90.8 %all-gather.20.cloned.1.call-start = ((), (), s32[]{:S(2)}) async-start(), calls=%async_computation.7 | async-start | bytes 2621440 | tf_op jit(solution)/shard_map/all_gather | solution.py:12
  268.7 113.8 %all-gather.22.cloned.1.call-start = ((), (), s32[]{:S(2)}) async-start(), calls=%async_computation.8 | async-start | bytes 2621440 | tf_op jit(solution)/shard_map/all_gather | solution.py:12
  269.7 136.9 %all-gather.18.cloned.1.call-start = ((), (), s32[]{:S(2)}) async-start(), calls=%async_computation.6 | async-start | bytes 2621440 | tf_op jit(solution)/shard_map/all_gather | solution.py:12
  270.7 160.1 %all-gather.10.cloned.1.call-start = ((), (), s32[]{:S(2)}) async-start(), calls=%async_computation.2 | async-start | bytes 2621440 | tf_op jit(solution)/shard_map/all_gather | solution.py:12
  271.6 183.4 %all-gather.16.cloned.1.call-start = ((), (), s32[]{:S(2)}) async-start(), calls=%async_computation.5 | async-start | bytes 2621440 | tf_op jit(solution)/shard_map/all_gather | solution.py:12
  272.6 264.5 %all-gather.26.cloned.1.call-start = ((), (), s32[]{:S(2)}) async-start(), calls=%async_computation.10 | async-start | bytes 5242880 | tf_op jit(solution)/shard_map/all_gather | solution.py:98
Sparse Core Ops, SparseCore 0:
  264.9 21.2 all-gather.23
  287.7 22.5 all-gather.11
  311.9 22.5 all-gather.13
  335.9 22.5 all-gather.19
  360.0 22.5 all-gather.21
  384.0 22.5 all-gather.17
  408.2 22.5 all-gather.9
  432.4 22.5 all-gather.15
  456.6 80.5 all-gather.25
